TPU v7x, 32 devices: a whole 2x2x4 slice. The times are simulated.
32 devices in a mesh: rep: 4 (over x, core), shard: 8 (over z, y).
Axes of the slice: x: 2, y: 2, z: 4, core: 2. Of those that a mesh axis runs over, the one named last changes fastest.
Arguments:
- hidden_acts: bfloat16 [24576, 128], P(('rep', 'shard')), may hold values from -6 to 6
- out_cotangent: bfloat16 [24576, 4096], P(('rep', 'shard')), may hold values from -0.0390625 to 0.0390625
- weight: bfloat16 [128, 4096], P('shard'), may hold values from -6 to 6
- first_moment: float32 [128, 4096], P('shard'), may hold values from -6 to 6
- second_moment: float32 [128, 4096], P('shard'), may hold values from 0.05 to 2
Outputs:
- new_weight: bfloat16 [128, 4096], replicated
- new_first: float32 [128, 4096], P('shard')
- new_second: float32 [128, 4096], P('shard')
All inputs are finite; a program needn't handle non-finite values.
Results may differ from a plain program's by a relative error of at most 0.0014.
Values may be sent and summed in bfloat16 or wider, within the bound.
No kernel may reach another device: no remote copies, remote signals or barrier semaphores. Data moves between devices by JAX's collectives and lax.ppermute only.
A program may use at most 128 MiB of HBM per device.

v0:
```python
import jax
import jax.numpy as jnp
from jax import lax
from jax.sharding import PartitionSpec as P


def adamw(weight, first_moment, second_moment, grad):
    corr_one = 0.9999734386011124
    corr_two = 0.0952078528
    new_first = 0.9 * first_moment + 0.1 * grad
    new_second = 0.999 * second_moment + 0.001 * grad * grad
    wfloat = weight.astype(jnp.float32)
    update = new_first / corr_one / (jnp.sqrt(new_second / corr_two) + 1e-08)
    new_weight = (wfloat - 0.05 * (update + 0.1 * wfloat)).astype(jnp.bfloat16)
    return (new_weight, new_first, new_second)


def contract(acts, cots):
    return lax.dot_general(acts, cots, (((0,), (0,)), ((), ())), preferred_element_type=jnp.float32)


def body(hidden_acts, out_cotangent, weight, first_moment, second_moment):
    rows_dev = weight.shape[0]
    tok_rows = hidden_acts.shape[0]
    rep_count = lax.axis_size("rep")
    shard_count = lax.axis_size("shard")
    quarter = rows_dev // rep_count
    ordered = hidden_acts.reshape(tok_rows, shard_count, rep_count, quarter)
    ordered = ordered.transpose(0, 2, 1, 3).reshape(tok_rows, shard_count * rows_dev)
    grad = lax.psum_scatter(
        contract(hidden_acts, out_cotangent), "shard", scatter_dimension=0, tiled=True
    )
    grad = lax.psum(grad.astype(jnp.bfloat16), "rep").astype(jnp.float32)
    new_w, new_m, new_v = adamw(weight, first_moment, second_moment, grad)
    weights_out = lax.all_gather(new_w, "shard", axis=0, tiled=True)
    return (weights_out, new_m, new_v)


def solution(mesh):
    return jax.shard_map(
        body,
        mesh=mesh,
        in_specs=(
            P(("rep", "shard"), None),
            P(("rep", "shard"), None),
            P("shard", None),
            P("shard", None),
            P("shard", None),
        ),
        out_specs=(P(), P("shard", None), P("shard", None)),
        check_vma=False,
    )
```

profile of v0, /device:TPU:0, one launch (start us, length us, event | category | flops | bytes accessed | tf_op | source)
XLA Modules:
  0.0 169.2 jit_solution(5244861371290595302)
XLA Ops:
  7.2 0.0 copy-start
  7.2 0.0 copy-start.2
  7.2 0.0 copy-start.1
  7.2 0.0 copy-start.3
  7.2 0.0 reduce-scatter.2.cloned.1.call-start
  7.3 0.8 copy-done
  8.1 5.1 %fusion.7 = f32[128,4096]{1,0:T(8,128)} fusion(bf16[768,128]{1,0:T(8,128)(2,1)S(1)} %copy-done, bf16[768,4096]{1,0:T(8,128)(2,1)} %param.6), kind=kOutput, calls=%fused_computation.9 | convolution fusion | flops 805306368 | bytes 8585216 | tf_op jit(solution)/shard_map/dot_general | solution.py:19
  13.2 0.0 reduce-scatter.2.cloned.1.call-update
  13.3 0.0 all-reduce.2.cloned.1.call-start
  13.3 70.6 %reduce-scatter.2.cloned.1.call-done = f32[16,4096]{1,0:T(8,128)} async-done(((f32[128,4096]{1,0:T(8,128)}), f32[16,4096]{1,0:T(8,128)}) %reduce-scatter.2.cloned.1.call-update) | async-done | bytes 262160 | tf_op jit(solution)/shard_map/reduce_scatter | solution.py:30
  84.0 1.6 convert_element_type.13
  85.6 0.0 all-reduce.2.cloned.1.call-update
  85.6 0.0 all-gather.2.cloned.1.call-start
  85.6 31.6 %all-reduce.2.cloned.1.call-done = bf16[16,4096]{1,0:T(8,128)(2,1)} async-done(((bf16[16,4096]{1,0:T(8,128)(2,1)}), bf16[16,4096]{1,0:T(8,128)(2,1)}) %all-reduce.2.cloned.1.call-update) | async-done | bytes 131088 | tf_op jit(solution)/shard_map/psum | solution.py:33
  117.3 0.0 copy-done.2
  117.3 0.0 copy-done.1
  117.3 0.0 copy-done.3
  117.3 1.9 %fusion.2 = (bf16[16,4096]{1,0:T(8,128)(2,1)}, f32[16,4096]{1,0:T(8,128)}, f32[16,4096]{1,0:T(8,128)}) fusion(bf16[16,4096]{1,0:T(8,128)(2,1)S(1)} %copy-done.3, bf16[16,4096]{1,0:T(8,128)(2,1)} %all-reduce.2.cloned.1.call-done, f32[16,4096]{1,0:T(8,128)S(1)} %copy-done.1, f32[16,4096]{1,0:T(8,128)S(1)} %copy-done.2), kind=kLoop, calls=%fused_computation.6 | loop fusion | flops 1179648 | bytes 1441792 | tf_op jit(solution)/shard_map/convert_element_type | solution.py:14
  119.2 0.0 all-gather.2.cloned.1.call-update
  119.2 41.2 %all-gather.2.cloned.1.call-done = bf16[128,4096]{1,0:T(8,128)(2,1)} async-done(((bf16[16,4096]{1,0:T(8,128)(2,1)}), bf16[128,4096]{1,0:T(8,128)(2,1)}) %all-gather.2.cloned.1.call-update) | async-done | bytes 1048592 | tf_op jit(solution)/shard_map/all_gather | solution.py:35
  160.4 2.3 %copy.10 = bf16[128,4096]{1,0:T(8,128)(2,1)} copy(bf16[128,4096]{1,0:T(8,128)(2,1)} %all-gather.2.cloned.1.call-done) | data formatting | bytes 2097152
Async XLA Ops:
  7.2 0.9 copy-start
  7.2 110.1 %copy-start.2 = (f32[16,4096]{1,0:T(8,128)S(1)}, f32[16,4096]{1,0:T(8,128)}, u32[]{:S(2)}) copy-start(f32[16,4096]{1,0:T(8,128)} %param.9) | copy-start | bytes 786436
  7.2 110.1 %copy-start.1 = (f32[16,4096]{1,0:T(8,128)S(1)}, f32[16,4096]{1,0:T(8,128)}, u32[]{:S(2)}) copy-start(f32[16,4096]{1,0:T(8,128)} %param.8) | copy-start | bytes 786436
  7.2 110.1 %copy-start.3 = (bf16[16,4096]{1,0:T(8,128)(2,1)S(1)}, bf16[16,4096]{1,0:T(8,128)(2,1)}, u32[]{:S(2)}) copy-start(bf16[16,4096]{1,0:T(8,128)(2,1)} %param.7) | copy-start | bytes 393220
  7.2 76.7 %reduce-scatter.2.cloned.1.call-start = ((), (), s32[]{:S(2)}) async-start(), calls=%async_computation.1 | async-start | bytes 2359296 | tf_op jit(solution)/shard_map/reduce_scatter | solution.py:30
  13.3 104.0 %all-reduce.2.cloned.1.call-start = ((), (), s32[]{:S(2)}) async-start(), calls=%async_computation.2 | async-start | bytes 262144 | tf_op jit(solution)/shard_map/psum | solution.py:33
  85.6 74.8 %all-gather.2.cloned.1.call-start = ((), (), s32[]{:S(2)}) async-start(), calls=%async_computation.3 | async-start | bytes 1179648 | tf_op jit(solution)/shard_map/all_gather | solution.py:35
Sparse Core Ops, SparseCore 0:
  13.4 70.5 reduce-scatter.1
  86.8 30.3 all-reduce.1
  120.2 40.1 all-gather.1
where the time goes:
time: 169 us
  waiting for transfers between devices  144 us (85%)
  between operations  13.8 us (8%)
  matrix products  5.14 us (3%)
  other arithmetic  3.48 us (2%)
  local copies, waits for them, and re-layouts  3.15 us (2%)
    reduce_scatter x1, waiting for transfers between devices, body(): lax.psum_scatter(contract(hidden_acts, out_cotangent), 'shard', scatter_d...  70.6 us
    all_gather x1, waiting for transfers between devices, body(): weights_out = lax.all_gather(new_w, 'shard', axis=0, tiled=True)  41.2 us
    psum x1, waiting for transfers between devices, body(): grad = lax.psum(grad.astype(jnp.bfloat16), 'rep').astype(jnp.float32)  31.6 us
    dot_general x1, matrix products, contract(): lax.dot_general(acts, cots, (((0,), (0,)), ((), ())), preferred_element_t...  5.14 us
  transfers between devices with their start and end apart: 3, of which 3 were waited for; matrix products, arithmetic and copies ran while one was open for 0% of the time, Pallas kernels for 0%

commit v1 on v0

v1 whole, which is shorter than its diff:
```python
import functools

import jax
import jax.numpy as jnp
from jax import lax
from jax.experimental import pallas as pl
from jax.experimental.pallas import tpu as pltpu
from jax.sharding import PartitionSpec as P

F32 = jnp.float32
BF16 = jnp.bfloat16


def adamw_moments(first_moment, second_moment, grad):
    new_first = 0.9 * first_moment + 0.1 * grad
    new_second = 0.999 * second_moment + 0.001 * grad * grad
    return new_first, new_second


def adamw_weight(weight, new_first, new_second):
    corr_one = 0.9999734386011124
    corr_two = 0.0952078528
    wfloat = weight.astype(F32)
    update = new_first / corr_one / (jnp.sqrt(new_second / corr_two) + 1e-08)
    return (wfloat - 0.05 * (update + 0.1 * wfloat)).astype(BF16)


def contract(acts, cots):
    return lax.dot_general(acts, cots, (((0,), (0,)), ((), ())), preferred_element_type=F32)


def in_vmem(kernel, out_shapes, *args):
    spec = pl.BlockSpec(memory_space=pltpu.VMEM)
    return pl.pallas_call(
        kernel,
        out_shape=out_shapes,
        in_specs=[spec] * len(args),
        out_specs=jax.tree.map(lambda _: spec, out_shapes),
        compiler_params=pltpu.CompilerParams(vmem_limit_bytes=48 * 1024 * 1024),
    )(*args)


def shape(dims, kind):
    return jax.ShapeDtypeStruct(dims, kind)


def split_kernel(rows, kept_ref, came_ref, own_ref, *piece_refs):
    me = lax.axis_index("shard")
    for k in range(len(piece_refs) + 1):
        at = pl.ds(pl.multiple_of((me ^ k) * rows, rows), rows)
        total = kept_ref[at, :] + came_ref[at, :].astype(F32)
        if k == 0:
            own_ref[...] = total
        else:
            piece_refs[k - 1][...] = total.astype(BF16)


def place(index):
    bits = lax.axis_size("rep").bit_length() - 1
    return sum(((index >> bit) & 1) << (bits - 1 - bit) for bit in range(bits))


def update_kernel(w_ref, m_ref, v_ref, own_ref, *refs):
    piece_refs, (new_w_ref, grad_ref) = refs[:-2], refs[-2:]
    me = lax.axis_index("rep")
    total = own_ref[...]
    for ref in piece_refs:
        total += ref[...].astype(F32)
    cols = total.shape[1]
    at = pl.ds(pl.multiple_of(place(me) * cols, cols), cols)
    sent = total.astype(BF16)
    new_m, new_v = adamw_moments(m_ref[:, at], v_ref[:, at], sent.astype(F32))
    new_w_ref[...] = adamw_weight(w_ref[:, at], new_m, new_v)
    grad_ref[...] = sent


def moments_kernel(m_ref, v_ref, *refs):
    grad_refs, (new_m_ref, new_v_ref) = refs[:-2], refs[-2:]
    me = lax.axis_index("rep")
    for k, ref in enumerate(grad_refs):
        cols = ref.shape[1]
        at = pl.ds(pl.multiple_of(place(me ^ k) * cols, cols), cols)
        new_m_ref[:, at], new_v_ref[:, at] = adamw_moments(m_ref[:, at], v_ref[:, at], ref[...].astype(F32))


def rows_kernel(*refs):
    piece_refs, out_ref = refs[:-1], refs[-1]
    me = lax.axis_index("shard")
    for k, ref in enumerate(piece_refs):
        rows = ref.shape[0]
        out_ref[pl.ds(pl.multiple_of((me ^ k) * rows, rows), rows), :] = ref[...]


def columns_kernel(bit, low_ref, high_ref, out_ref):
    mine = (lax.axis_index("rep") >> bit) & 1
    cols = low_ref.shape[1]
    out_ref[:, pl.ds(pl.multiple_of(mine * cols, cols), cols)] = low_ref[...]
    out_ref[:, pl.ds(pl.multiple_of((1 - mine) * cols, cols), cols)] = high_ref[...]


def swap(value, axis, k):
    return lax.ppermute(value, axis, [(i, i ^ k) for i in range(lax.axis_size(axis))])


def body(hidden_acts, out_cotangent, weight, first_moment, second_moment):
    rows_dev, width = weight.shape
    rep_count = lax.axis_size("rep")
    shard_count = lax.axis_size("shard")
    all_rows = hidden_acts.shape[1]
    bits = rep_count.bit_length() - 1
    rep = lax.axis_index("rep")

    half = width // 2
    mine = rep & 1
    cut = lambda value, index, size: lax.dynamic_slice_in_dim(value, index * size, size, 1)
    away = contract(hidden_acts, cut(out_cotangent, 1 - mine, half)).astype(BF16)
    came = swap(away, "rep", 1)
    kept = contract(hidden_acts, cut(out_cotangent, mine, half))
    for bit in range(1, bits):
        total = kept + came.astype(F32)
        half //= 2
        mine = (rep >> bit) & 1
        came = swap(cut(total, 1 - mine, half).astype(BF16), "rep", 1 << bit)
        kept = cut(total, mine, half)

    cols = half
    own, *pieces = in_vmem(
        functools.partial(split_kernel, rows_dev),
        [shape((rows_dev, cols), F32)] + [shape((rows_dev, cols), BF16)] * (shard_count - 1),
        kept, came,
    )
    pieces = [swap(piece, "shard", k + 1) for k, piece in enumerate(pieces)]
    new_w, grad = in_vmem(
        update_kernel,
        [shape((rows_dev, cols), BF16)] * 2,
        weight, first_moment, second_moment, own, *pieces,
    )
    w_pieces = [new_w] + [swap(new_w, "shard", k) for k in range(1, shard_count)]
    grads = [grad] + [swap(grad, "rep", k) for k in range(1, rep_count)]
    part = in_vmem(rows_kernel, shape((all_rows, cols), BF16), *w_pieces)
    for bit in reversed(range(bits)):
        other = swap(part, "rep", 1 << bit)
        part = in_vmem(
            functools.partial(columns_kernel, bit),
            shape((all_rows, 2 * part.shape[1]), BF16), part, other,
        )
    new_m, new_v = in_vmem(
        moments_kernel,
        [shape((rows_dev, width), F32)] * 2,
        first_moment, second_moment, *grads,
    )
    return part, new_m, new_v


def solution(mesh):
    return jax.shard_map(
        body,
        mesh=mesh,
        in_specs=(
            P(("rep", "shard"), None),
            P(("rep", "shard"), None),
            P("shard", None),
            P("shard", None),
            P("shard", None),
        ),
        out_specs=(P(), P("shard", None), P("shard", None)),
        check_vma=False,
    )
```

time: 169 us -> 64.3 us (0.38)
  waiting for transfers between devices: 144 us -> 25.6 us
  starting transfers between devices: 0.12 us -> 29.6 us
  between operations: 13.8 us -> 0.73 us
  other arithmetic: 3.48 us -> 0 us
  Pallas kernels: 0 us -> 2.15 us
  local copies, waits for them, and re-layouts: 3.15 us -> 1 us
    reduce_scatter x1 -> x0, waiting for transfers between devices: 70.6 us -> none  [body(): lax.psum_scatter(contract(hidden_acts, out_cotangent), 'shard', scatter_d...]
    all_gather x1 -> x0, waiting for transfers between devices: 41.2 us -> none  [body(): weights_out = lax.all_gather(new_w, 'shard', axis=0, tiled=True)]
    psum x1 -> x0, waiting for transfers between devices: 31.6 us -> none  [body(): grad = lax.psum(grad.astype(jnp.bfloat16), 'rep').astype(jnp.float32)]
    ppermute x0 -> x21, starting transfers between devices: none -> 29.6 us  [swap(): lax.ppermute(value, axis, [(i, i ^ k) for i in range(lax.axis_size(axis))])]
    ppermute x0 -> x21, waiting for transfers between devices: none -> 25.6 us  [swap(): lax.ppermute(value, axis, [(i, i ^ k) for i in range(lax.axis_size(axis))])]
    convert_element_type x2 -> x0, other arithmetic: 3.48 us -> none  [the longest x1 1.87 us: adamw(): new_weight = (wfloat - 0.05 * (update + 0.1 * wfloat)).astype(jnp.bfloat16)]
    unnamed x9 -> x8, local copies, waits for them, and re-layouts: 3.15 us -> 0.93 us
    pallas_call x0 -> x6, Pallas kernels: none -> 2.15 us  [in_vmem(): pl.pallas_call(kernel, out_shape=out_shapes, in_specs=[spec] * len(args),...]
  transfers between devices with their start and end apart: 3 -> 21, of which waited for: 3 -> 10; matrix products, arithmetic and copies ran while one was open for 0% -> 0% of each run, Pallas kernels for 0% -> 1%
where the time goes in v1:
time: 64.3 us; the launch traced here: 64.1 us
  starting transfers between devices  29.6 us (46%)
  waiting for transfers between devices  25.6 us (40%)
  matrix products  5.1 us (8%)
  Pallas kernels  2.15 us (3%)
  local copies, waits for them, and re-layouts  1 us (2%)
  between operations  0.73 us (1%)
    ppermute x21, starting transfers between devices, swap(): lax.ppermute(value, axis, [(i, i ^ k) for i in range(lax.axis_size(axis))])  29.6 us
    ppermute x21, waiting for transfers between devices, swap(): lax.ppermute(value, axis, [(i, i ^ k) for i in range(lax.axis_size(axis))])  25.6 us
    dot_general x2, matrix products, contract(): lax.dot_general(acts, cots, (((0,), (0,)), ((), ())), preferred_element_t...  5.1 us
    pallas_call x6, Pallas kernels, in_vmem(): pl.pallas_call(kernel, out_shape=out_shapes, in_specs=[spec] * len(args),...  2.15 us
  transfers between devices with their start and end apart: 21, of which 10 were waited for; matrix products, arithmetic and copies ran while one was open for 0% of the time, Pallas kernels for 1%

profile of v1, /device:TPU:0, one launch (start us, length us, event | category | flops | bytes accessed | tf_op | source)
XLA Modules:
  0.0 64.1 jit_solution(3303240285402015143)
XLA Ops:
  0.7 0.9 %copy-done = bf16[768,128]{1,0:T(8,128)(2,1)S(1)} copy-done((bf16[768,128]{1,0:T(8,128)(2,1)S(1)}, bf16[768,128]{1,0:T(8,128)(2,1)}, u32[]{:S(2)}) %copy-start) | copy-done | bytes 196632
  1.6 2.6 %fusion.10 = bf16[128,2048]{1,0:T(8,128)(2,1)S(1)} fusion(bf16[768,128]{1,0:T(8,128)(2,1)S(1)} %copy-done, bf16[768,4096]{1,0:T(8,128)(2,1)} %param.6, s32[]{:T(128)S(6)} %select_n.13), kind=kOutput, calls=%fused_computation.6 | convolution fusion | flops 402915328 | bytes 3866628 | tf_op jit(solution)/shard_map/dot_general | solution.py:29
  4.7 1.5 %collective-permute-done = bf16[128,2048]{1,0:T(8,128)(2,1)S(1)} collective-permute-done((bf16[128,2048]{1,0:T(8,128)(2,1)S(1)}, bf16[128,2048]{1,0:T(8,128)(2,1)S(1)}, u32[]{:S(2)}, u32[]{:S(2)}) %collective-permute-start) | collective-permute-done | bytes 524320 | tf_op jit(solution)/shard_map/ppermute | solution.py:102
  6.2 2.5 %convert_add_fusion = f32[128,2048]{1,0:T(8,128)S(1)} fusion(bf16[128,2048]{1,0:T(8,128)(2,1)S(1)} %collective-permute-done, bf16[768,128]{1,0:T(8,128)(2,1)S(1)} %copy-done, bf16[768,4096]{1,0:T(8,128)(2,1)} %param.6, s32[]{:T(128)S(6)} %select_n.12), kind=kOutput, calls=%fused_computation.7 | convolution fusion | flops 403177472 | bytes 4915204 | tf_op jit(solution)/shard_map/dot_general | solution.py:29
  8.8 2.9 %collective-permute-start.1 = (bf16[128,1024]{1,0:T(8,128)(2,1)S(1)}, bf16[128,1024]{1,0:T(8,128)(2,1)S(1)}, u32[]{:S(2)}, u32[]{:S(2)}) collective-permute-start(bf16[128,1024]{1,0:T(8,128)(2,1)S(1)} %dynamic-slice_convert_fusion), channel_id=1, source_target_pairs={{0,16},{8,24},{16,0},{24,8},{1,17},{9,25},{17,1},{25,9},{2,18},{10... | collective-permute-start | bytes 786440 | tf_op jit(solution)/shard_map/ppermute | solution.py:102
  11.8 6.6 %collective-permute-done.1.came_ref = bf16[128,1024]{1,0:T(8,128)(2,1)S(1)} collective-permute-done((bf16[128,1024]{1,0:T(8,128)(2,1)S(1)}, bf16[128,1024]{1,0:T(8,128)(2,1)S(1)}, u32[]{:S(2)}, u32[]{:S(2)}) %collective-permute-start.1) | collective-permute-done | bytes 262176 | tf_op jit(solution)/shard_map/ppermute | solution.py:102
  18.4 1.8 %collective-permute-start.2 = (bf16[16,1024]{1,0:T(8,128)(2,1)S(1)}, bf16[16,1024]{1,0:T(8,128)(2,1)S(1)}, u32[]{:S(2)}, u32[]{:S(2)}) collective-permute-start(bf16[16,1024]{1,0:T(8,128)(2,1)S(1)} %get-tuple-element.16), channel_id=1, source_target_pairs={{0,1},{1,0},{2,3},{3,2},{4,5},{5,4},{6,7},{7,6},{8,9},{9,8},{10,11... | collective-permute-start | bytes 98312 | tf_op jit(solution)/shard_map/ppermute | solution.py:102
  20.2 1.6 %collective-permute-start.3 = (bf16[16,1024]{1,0:T(8,128)(2,1)S(1)}, bf16[16,1024]{1,0:T(8,128)(2,1)S(1)}, u32[]{:S(2)}, u32[]{:S(2)}) collective-permute-start(bf16[16,1024]{1,0:T(8,128)(2,1)S(1)} %get-tuple-element.17), channel_id=1, source_target_pairs={{0,2},{1,3},{2,0},{3,1},{4,6},{5,7},{6,4},{7,5},{8,10},{9,11},{10,... | collective-permute-start | bytes 98312 | tf_op jit(solution)/shard_map/ppermute | solution.py:102
  21.9 2.8 %collective-permute-start.5 = (bf16[16,1024]{1,0:T(8,128)(2,1)S(1)}, bf16[16,1024]{1,0:T(8,128)(2,1)S(1)}, u32[]{:S(2)}, u32[]{:S(2)}) collective-permute-start(bf16[16,1024]{1,0:T(8,128)(2,1)S(1)} %get-tuple-element.19), channel_id=1, source_target_pairs={{0,4},{1,5},{2,6},{3,7},{4,0},{5,1},{6,2},{7,3},{8,12},{9,13},{10,... | collective-permute-start | bytes 98312 | tf_op jit(solution)/shard_map/ppermute | solution.py:102
  24.7 1.3 %collective-permute-start.6 = (bf16[16,1024]{1,0:T(8,128)(2,1)S(1)}, bf16[16,1024]{1,0:T(8,128)(2,1)S(1)}, u32[]{:S(2)}, u32[]{:S(2)}) collective-permute-start(bf16[16,1024]{1,0:T(8,128)(2,1)S(1)} %get-tuple-element.20), channel_id=1, source_target_pairs={{0,5},{1,4},{2,7},{3,6},{4,1},{5,0},{6,3},{7,2},{8,13},{9,12},{10,... | collective-permute-start | bytes 98312 | tf_op jit(solution)/shard_map/ppermute | solution.py:102
  26.0 3.6 %collective-permute-start.7 = (bf16[16,1024]{1,0:T(8,128)(2,1)S(1)}, bf16[16,1024]{1,0:T(8,128)(2,1)S(1)}, u32[]{:S(2)}, u32[]{:S(2)}) collective-permute-start(bf16[16,1024]{1,0:T(8,128)(2,1)S(1)} %get-tuple-element.21), channel_id=1, source_target_pairs={{0,6},{1,7},{2,4},{3,5},{4,2},{5,3},{6,0},{7,1},{8,14},{9,15},{10,... | collective-permute-start | bytes 98312 | tf_op jit(solution)/shard_map/ppermute | solution.py:102
  30.5 1.8 %collective-permute-done.7.refs_5_ = bf16[16,1024]{1,0:T(8,128)(2,1)S(1)} collective-permute-done((bf16[16,1024]{1,0:T(8,128)(2,1)S(1)}, bf16[16,1024]{1,0:T(8,128)(2,1)S(1)}, u32[]{:S(2)}, u32[]{:S(2)}) %collective-permute-start.7) | collective-permute-done | bytes 32800 | tf_op jit(solution)/shard_map/ppermute | solution.py:102
  32.2 4.0 %collective-permute-done.8.refs_6_ = bf16[16,1024]{1,0:T(8,128)(2,1)S(1)} collective-permute-done((bf16[16,1024]{1,0:T(8,128)(2,1)S(1)}, bf16[16,1024]{1,0:T(8,128)(2,1)S(1)}, u32[]{:S(2)}, u32[]{:S(2)}) %collective-permute-start.8) | collective-permute-done | bytes 32800 | tf_op jit(solution)/shard_map/ppermute | solution.py:102
  37.1 2.8 %collective-permute-start.11 = (bf16[16,1024]{1,0:T(8,128)(2,1)S(1)}, bf16[16,1024]{1,0:T(8,128)(2,1)S(1)}, u32[]{:S(2)}, u32[]{:S(2)}) collective-permute-start(bf16[16,1024]{1,0:T(8,128)(2,1)S(1)} %get-tuple-element.23.refs_0_), channel_id=1, source_target_pairs={{0,3},{1,2},{2,1},{3,0},{4,7},{5,6},{6,5},{7,4},{8,11},{9,10},{10,... | collective-permute-start | bytes 98312 | tf_op jit(solution)/shard_map/ppermute | solution.py:102
  39.9 3.0 %collective-permute-start.13 = (bf16[16,1024]{1,0:T(8,128)(2,1)S(1)}, bf16[16,1024]{1,0:T(8,128)(2,1)S(1)}, u32[]{:S(2)}, u32[]{:S(2)}) collective-permute-start(bf16[16,1024]{1,0:T(8,128)(2,1)S(1)} %get-tuple-element.23.refs_0_), channel_id=1, source_target_pairs={{0,5},{1,4},{2,7},{3,6},{4,1},{5,0},{6,3},{7,2},{8,13},{9,12},{10,... | collective-permute-start | bytes 98312 | tf_op jit(solution)/shard_map/ppermute | solution.py:102
  43.3 4.3 %collective-permute-start.15 = (bf16[16,1024]{1,0:T(8,128)(2,1)S(1)}, bf16[16,1024]{1,0:T(8,128)(2,1)S(1)}, u32[]{:S(2)}, u32[]{:S(2)}) collective-permute-start(bf16[16,1024]{1,0:T(8,128)(2,1)S(1)} %get-tuple-element.23.refs_0_), channel_id=1, source_target_pairs={{0,7},{1,6},{2,5},{3,4},{4,3},{5,2},{6,1},{7,0},{8,15},{9,14},{10,... | collective-permute-start | bytes 98312 | tf_op jit(solution)/shard_map/ppermute | solution.py:102
  47.6 1.1 %collective-permute-done.14.refs_6_ = bf16[16,1024]{1,0:T(8,128)(2,1)S(1)} collective-permute-done((bf16[16,1024]{1,0:T(8,128)(2,1)S(1)}, bf16[16,1024]{1,0:T(8,128)(2,1)S(1)}, u32[]{:S(2)}, u32[]{:S(2)}) %collective-permute-start.14) | collective-permute-done | bytes 32800 | tf_op jit(solution)/shard_map/ppermute | solution.py:102
  48.7 1.3 %collective-permute-done.15.refs_7_ = bf16[16,1024]{1,0:T(8,128)(2,1)S(1)} collective-permute-done((bf16[16,1024]{1,0:T(8,128)(2,1)S(1)}, bf16[16,1024]{1,0:T(8,128)(2,1)S(1)}, u32[]{:S(2)}, u32[]{:S(2)}) %collective-permute-start.15) | collective-permute-done | bytes 32800 | tf_op jit(solution)/shard_map/ppermute | solution.py:102
  50.0 1.6 %collective-permute-start.16 = (bf16[128,1024]{1,0:T(8,128)(2,1)S(1)}, bf16[128,1024]{1,0:T(8,128)(2,1)S(1)}, u32[]{:S(2)}, u32[]{:S(2)}) collective-permute-start(bf16[128,1024]{1,0:T(8,128)(2,1)S(1)} %shard_map.78.low_ref), channel_id=1, source_target_pairs={{0,16},{8,24},{16,0},{24,8},{1,17},{9,25},{17,1},{25,9},{2,18},{10... | collective-permute-start | bytes 786440 | tf_op jit(solution)/shard_map/ppermute | solution.py:102
  51.5 4.9 %collective-permute-done.16.high_ref = bf16[128,1024]{1,0:T(8,128)(2,1)S(1)} collective-permute-done((bf16[128,1024]{1,0:T(8,128)(2,1)S(1)}, bf16[128,1024]{1,0:T(8,128)(2,1)S(1)}, u32[]{:S(2)}, u32[]{:S(2)}) %collective-permute-start.16) | collective-permute-done | bytes 262176 | tf_op jit(solution)/shard_map/ppermute | solution.py:102
  57.0 1.5 %collective-permute-start.19 = (bf16[16,1024]{1,0:T(8,128)(2,1)S(1)}, bf16[16,1024]{1,0:T(8,128)(2,1)S(1)}, u32[]{:S(2)}, u32[]{:S(2)}) collective-permute-start(bf16[16,1024]{1,0:T(8,128)(2,1)S(1)} %get-tuple-element.24.refs_0_), channel_id=1, source_target_pairs={{0,16},{8,24},{16,0},{24,8},{1,17},{9,25},{17,1},{25,9},{2,18},{10... | collective-permute-start | bytes 98312 | tf_op jit(solution)/shard_map/ppermute | solution.py:102
  58.5 2.4 %collective-permute-done.19.refs_2_ = bf16[16,1024]{1,0:T(8,128)(2,1)S(1)} collective-permute-done((bf16[16,1024]{1,0:T(8,128)(2,1)S(1)}, bf16[16,1024]{1,0:T(8,128)(2,1)S(1)}, u32[]{:S(2)}, u32[]{:S(2)}) %collective-permute-start.19) | collective-permute-done | bytes 32800 | tf_op jit(solution)/shard_map/ppermute | solution.py:102
  61.0 1.2 %collective-permute-done.20.refs_3_ = bf16[16,1024]{1,0:T(8,128)(2,1)S(1)} collective-permute-done((bf16[16,1024]{1,0:T(8,128)(2,1)S(1)}, bf16[16,1024]{1,0:T(8,128)(2,1)S(1)}, u32[]{:S(2)}, u32[]{:S(2)}) %collective-permute-start.20) | collective-permute-done | bytes 32800 | tf_op jit(solution)/shard_map/ppermute | solution.py:102
  63.1 1.1 %shard_map.80 = bf16[128,4096]{1,0:T(8,128)(2,1)} custom-call(bf16[128,2048]{1,0:T(8,128)(2,1)S(1)} %shard_map.79.low_ref, bf16[128,2048]{1,0:T(8,128)(2,1)S(1)} %collective-permute-done.17.high_ref), custom_call_target="tpu_custom_call" | custom-call | tf_op jit(solution)/shard_map/pallas_call | solution.py:34
  (36 shorter events, 4.3 us)
Async XLA Ops:
  1.6 34.7 %copy-start.1 = (f32[16,4096]{1,0:T(8,128)S(1)}, f32[16,4096]{1,0:T(8,128)}, u32[]{:S(2)}) copy-start(f32[16,4096]{1,0:T(8,128)} %m_ref.3) | copy-start | bytes 786436
  1.6 34.7 %copy-start.2 = (f32[16,4096]{1,0:T(8,128)S(1)}, f32[16,4096]{1,0:T(8,128)}, u32[]{:S(2)}) copy-start(f32[16,4096]{1,0:T(8,128)} %v_ref.3) | copy-start | bytes 786436
  1.6 34.7 %copy-start.3 = (bf16[16,4096]{1,0:T(8,128)(2,1)S(1)}, bf16[16,4096]{1,0:T(8,128)(2,1)}, u32[]{:S(2)}) copy-start(bf16[16,4096]{1,0:T(8,128)(2,1)} %w_ref.1) | copy-start | bytes 393220
  4.2 2.1 %collective-permute-start = (bf16[128,2048]{1,0:T(8,128)(2,1)S(1)}, bf16[128,2048]{1,0:T(8,128)(2,1)S(1)}, u32[]{:S(2)}, u32[]{:S(2)}) collective-permute-start(bf16[128,2048]{1,0:T(8,128)(2,1)S(1)} %fusion.10), channel_id=1, source_target_pairs={{0,8},{8,0},{16,24},{24,16},{1,9},{9,1},{17,25},{25,17},{2,10},{10... | collective-permute-start | bytes 1572872 | tf_op jit(solution)/shard_map/ppermute | solution.py:102
  8.8 9.5 %collective-permute-start.1 = (bf16[128,1024]{1,0:T(8,128)(2,1)S(1)}, bf16[128,1024]{1,0:T(8,128)(2,1)S(1)}, u32[]{:S(2)}, u32[]{:S(2)}) collective-permute-start(bf16[128,1024]{1,0:T(8,128)(2,1)S(1)} %dynamic-slice_convert_fusion), channel_id=1, source_target_pairs={{0,16},{8,24},{16,0},{24,8},{1,17},{9,25},{17,1},{25,9},{2,18},{10... | collective-permute-start | bytes 786440 | tf_op jit(solution)/shard_map/ppermute | solution.py:102
  18.4 7.7 %collective-permute-start.2 = (bf16[16,1024]{1,0:T(8,128)(2,1)S(1)}, bf16[16,1024]{1,0:T(8,128)(2,1)S(1)}, u32[]{:S(2)}, u32[]{:S(2)}) collective-permute-start(bf16[16,1024]{1,0:T(8,128)(2,1)S(1)} %get-tuple-element.16), channel_id=1, source_target_pairs={{0,1},{1,0},{2,3},{3,2},{4,5},{5,4},{6,7},{7,6},{8,9},{9,8},{10,11... | collective-permute-start | bytes 98312 | tf_op jit(solution)/shard_map/ppermute | solution.py:102
  20.2 9.5 %collective-permute-start.3 = (bf16[16,1024]{1,0:T(8,128)(2,1)S(1)}, bf16[16,1024]{1,0:T(8,128)(2,1)S(1)}, u32[]{:S(2)}, u32[]{:S(2)}) collective-permute-start(bf16[16,1024]{1,0:T(8,128)(2,1)S(1)} %get-tuple-element.17), channel_id=1, source_target_pairs={{0,2},{1,3},{2,0},{3,1},{4,6},{5,7},{6,4},{7,5},{8,10},{9,11},{10,... | collective-permute-start | bytes 98312 | tf_op jit(solution)/shard_map/ppermute | solution.py:102
  21.8 7.9 %collective-permute-start.4 = (bf16[16,1024]{1,0:T(8,128)(2,1)S(1)}, bf16[16,1024]{1,0:T(8,128)(2,1)S(1)}, u32[]{:S(2)}, u32[]{:S(2)}) collective-permute-start(bf16[16,1024]{1,0:T(8,128)(2,1)S(1)} %get-tuple-element.18), channel_id=1, source_target_pairs={{0,3},{1,2},{2,1},{3,0},{4,7},{5,6},{6,5},{7,4},{8,11},{9,10},{10,... | collective-permute-start | bytes 98312 | tf_op jit(solution)/shard_map/ppermute | solution.py:102
  21.9 7.8 %collective-permute-start.5 = (bf16[16,1024]{1,0:T(8,128)(2,1)S(1)}, bf16[16,1024]{1,0:T(8,128)(2,1)S(1)}, u32[]{:S(2)}, u32[]{:S(2)}) collective-permute-start(bf16[16,1024]{1,0:T(8,128)(2,1)S(1)} %get-tuple-element.19), channel_id=1, source_target_pairs={{0,4},{1,5},{2,6},{3,7},{4,0},{5,1},{6,2},{7,3},{8,12},{9,13},{10,... | collective-permute-start | bytes 98312 | tf_op jit(solution)/shard_map/ppermute | solution.py:102
  24.7 5.7 %collective-permute-start.6 = (bf16[16,1024]{1,0:T(8,128)(2,1)S(1)}, bf16[16,1024]{1,0:T(8,128)(2,1)S(1)}, u32[]{:S(2)}, u32[]{:S(2)}) collective-permute-start(bf16[16,1024]{1,0:T(8,128)(2,1)S(1)} %get-tuple-element.20), channel_id=1, source_target_pairs={{0,5},{1,4},{2,7},{3,6},{4,1},{5,0},{6,3},{7,2},{8,13},{9,12},{10,... | collective-permute-start | bytes 98312 | tf_op jit(solution)/shard_map/ppermute | solution.py:102
  26.0 6.2 %collective-permute-start.7 = (bf16[16,1024]{1,0:T(8,128)(2,1)S(1)}, bf16[16,1024]{1,0:T(8,128)(2,1)S(1)}, u32[]{:S(2)}, u32[]{:S(2)}) collective-permute-start(bf16[16,1024]{1,0:T(8,128)(2,1)S(1)} %get-tuple-element.21), channel_id=1, source_target_pairs={{0,6},{1,7},{2,4},{3,5},{4,2},{5,3},{6,0},{7,1},{8,14},{9,15},{10,... | collective-permute-start | bytes 98312 | tf_op jit(solution)/shard_map/ppermute | solution.py:102
  29.7 6.6 %collective-permute-start.8 = (bf16[16,1024]{1,0:T(8,128)(2,1)S(1)}, bf16[16,1024]{1,0:T(8,128)(2,1)S(1)}, u32[]{:S(2)}, u32[]{:S(2)}) collective-permute-start(bf16[16,1024]{1,0:T(8,128)(2,1)S(1)} %get-tuple-element.22), channel_id=1, source_target_pairs={{0,7},{1,6},{2,5},{3,4},{4,3},{5,2},{6,1},{7,0},{8,15},{9,14},{10,... | collective-permute-start | bytes 98312 | tf_op jit(solution)/shard_map/ppermute | solution.py:102
  36.4 6.6 %collective-permute-start.9 = (bf16[16,1024]{1,0:T(8,128)(2,1)S(1)}, bf16[16,1024]{1,0:T(8,128)(2,1)S(1)}, u32[]{:S(2)}, u32[]{:S(2)}) collective-permute-start(bf16[16,1024]{1,0:T(8,128)(2,1)S(1)} %get-tuple-element.23.refs_0_), channel_id=1, source_target_pairs={{0,1},{1,0},{2,3},{3,2},{4,5},{5,4},{6,7},{7,6},{8,9},{9,8},{10,11... | collective-permute-start | bytes 98312 | tf_op jit(solution)/shard_map/ppermute | solution.py:102
  37.1 6.2 %collective-permute-start.10 = (bf16[16,1024]{1,0:T(8,128)(2,1)S(1)}, bf16[16,1024]{1,0:T(8,128)(2,1)S(1)}, u32[]{:S(2)}, u32[]{:S(2)}) collective-permute-start(bf16[16,1024]{1,0:T(8,128)(2,1)S(1)} %get-tuple-element.23.refs_0_), channel_id=1, source_target_pairs={{0,2},{1,3},{2,0},{3,1},{4,6},{5,7},{6,4},{7,5},{8,10},{9,11},{10,... | collective-permute-start | bytes 98312 | tf_op jit(solution)/shard_map/ppermute | solution.py:102
  37.1 10.5 %collective-permute-start.11 = (bf16[16,1024]{1,0:T(8,128)(2,1)S(1)}, bf16[16,1024]{1,0:T(8,128)(2,1)S(1)}, u32[]{:S(2)}, u32[]{:S(2)}) collective-permute-start(bf16[16,1024]{1,0:T(8,128)(2,1)S(1)} %get-tuple-element.23.refs_0_), channel_id=1, source_target_pairs={{0,3},{1,2},{2,1},{3,0},{4,7},{5,6},{6,5},{7,4},{8,11},{9,10},{10,... | collective-permute-start | bytes 98312 | tf_op jit(solution)/shard_map/ppermute | solution.py:102
  39.9 7.7 %collective-permute-start.12 = (bf16[16,1024]{1,0:T(8,128)(2,1)S(1)}, bf16[16,1024]{1,0:T(8,128)(2,1)S(1)}, u32[]{:S(2)}, u32[]{:S(2)}) collective-permute-start(bf16[16,1024]{1,0:T(8,128)(2,1)S(1)} %get-tuple-element.23.refs_0_), channel_id=1, source_target_pairs={{0,4},{1,5},{2,6},{3,7},{4,0},{5,1},{6,2},{7,3},{8,12},{9,13},{10,... | collective-permute-start | bytes 98312 | tf_op jit(solution)/shard_map/ppermute | solution.py:102
  39.9 7.7 %collective-permute-start.13 = (bf16[16,1024]{1,0:T(8,128)(2,1)S(1)}, bf16[16,1024]{1,0:T(8,128)(2,1)S(1)}, u32[]{:S(2)}, u32[]{:S(2)}) collective-permute-start(bf16[16,1024]{1,0:T(8,128)(2,1)S(1)} %get-tuple-element.23.refs_0_), channel_id=1, source_target_pairs={{0,5},{1,4},{2,7},{3,6},{4,1},{5,0},{6,3},{7,2},{8,13},{9,12},{10,... | collective-permute-start | bytes 98312 | tf_op jit(solution)/shard_map/ppermute | solution.py:102
  43.0 5.7 %collective-permute-start.14 = (bf16[16,1024]{1,0:T(8,128)(2,1)S(1)}, bf16[16,1024]{1,0:T(8,128)(2,1)S(1)}, u32[]{:S(2)}, u32[]{:S(2)}) collective-permute-start(bf16[16,1024]{1,0:T(8,128)(2,1)S(1)} %get-tuple-element.23.refs_0_), channel_id=1, source_target_pairs={{0,6},{1,7},{2,4},{3,5},{4,2},{5,3},{6,0},{7,1},{8,14},{9,15},{10,... | collective-permute-start | bytes 98312 | tf_op jit(solution)/shard_map/ppermute | solution.py:102
  43.3 6.6 %collective-permute-start.15 = (bf16[16,1024]{1,0:T(8,128)(2,1)S(1)}, bf16[16,1024]{1,0:T(8,128)(2,1)S(1)}, u32[]{:S(2)}, u32[]{:S(2)}) collective-permute-start(bf16[16,1024]{1,0:T(8,128)(2,1)S(1)} %get-tuple-element.23.refs_0_), channel_id=1, source_target_pairs={{0,7},{1,6},{2,5},{3,4},{4,3},{5,2},{6,1},{7,0},{8,15},{9,14},{10,... | collective-permute-start | bytes 98312 | tf_op jit(solution)/shard_map/ppermute | solution.py:102
  50.0 6.4 %collective-permute-start.16 = (bf16[128,1024]{1,0:T(8,128)(2,1)S(1)}, bf16[128,1024]{1,0:T(8,128)(2,1)S(1)}, u32[]{:S(2)}, u32[]{:S(2)}) collective-permute-start(bf16[128,1024]{1,0:T(8,128)(2,1)S(1)} %shard_map.78.low_ref), channel_id=1, source_target_pairs={{0,16},{8,24},{16,0},{24,8},{1,17},{9,25},{17,1},{25,9},{2,18},{10... | collective-permute-start | bytes 786440 | tf_op jit(solution)/shard_map/ppermute | solution.py:102
  56.5 6.6 %collective-permute-start.17 = (bf16[128,2048]{1,0:T(8,128)(2,1)S(1)}, bf16[128,2048]{1,0:T(8,128)(2,1)S(1)}, u32[]{:S(2)}, u32[]{:S(2)}) collective-permute-start(bf16[128,2048]{1,0:T(8,128)(2,1)S(1)} %shard_map.79.low_ref), channel_id=1, source_target_pairs={{0,8},{8,0},{16,24},{24,16},{1,9},{9,1},{17,25},{25,17},{2,10},{10... | collective-permute-start | bytes 1572872 | tf_op jit(solution)/shard_map/ppermute | solution.py:102
  56.5 2.0 %collective-permute-start.18 = (bf16[16,1024]{1,0:T(8,128)(2,1)S(1)}, bf16[16,1024]{1,0:T(8,128)(2,1)S(1)}, u32[]{:S(2)}, u32[]{:S(2)}) collective-permute-start(bf16[16,1024]{1,0:T(8,128)(2,1)S(1)} %get-tuple-element.24.refs_0_), channel_id=1, source_target_pairs={{0,8},{8,0},{16,24},{24,16},{1,9},{9,1},{17,25},{25,17},{2,10},{10... | collective-permute-start | bytes 98312 | tf_op jit(solution)/shard_map/ppermute | solution.py:102
  57.0 3.9 %collective-permute-start.19 = (bf16[16,1024]{1,0:T(8,128)(2,1)S(1)}, bf16[16,1024]{1,0:T(8,128)(2,1)S(1)}, u32[]{:S(2)}, u32[]{:S(2)}) collective-permute-start(bf16[16,1024]{1,0:T(8,128)(2,1)S(1)} %get-tuple-element.24.refs_0_), channel_id=1, source_target_pairs={{0,16},{8,24},{16,0},{24,8},{1,17},{9,25},{17,1},{25,9},{2,18},{10... | collective-permute-start | bytes 98312 | tf_op jit(solution)/shard_map/ppermute | solution.py:102
  58.5 3.7 %collective-permute-start.20 = (bf16[16,1024]{1,0:T(8,128)(2,1)S(1)}, bf16[16,1024]{1,0:T(8,128)(2,1)S(1)}, u32[]{:S(2)}, u32[]{:S(2)}) collective-permute-start(bf16[16,1024]{1,0:T(8,128)(2,1)S(1)} %get-tuple-element.24.refs_0_), channel_id=1, source_target_pairs={{0,24},{8,16},{16,8},{24,0},{1,25},{9,17},{17,9},{25,1},{2,26},{10... | collective-permute-start | bytes 98312 | tf_op jit(solution)/shard_map/ppermute | solution.py:102
  (1 other events, 0.9 us)

commit v2 on v0

v2 whole, which is shorter than its diff:
```python
import functools

import jax
import jax.numpy as jnp
from jax import lax
from jax.experimental import pallas as pl
from jax.experimental.pallas import tpu as pltpu
from jax.sharding import PartitionSpec as P

F32 = jnp.float32
BF16 = jnp.bfloat16
CHUNK = 512


def adamw_moments(first_moment, second_moment, grad):
    new_first = 0.9 * first_moment + 0.1 * grad
    new_second = 0.999 * second_moment + 0.001 * grad * grad
    return new_first, new_second


def adamw_weight(weight, new_first, new_second):
    corr_one = 0.9999734386011124
    corr_two = 0.0952078528
    wfloat = weight.astype(F32)
    update = new_first / corr_one / (jnp.sqrt(new_second / corr_two) + 1e-08)
    return (wfloat - 0.05 * (update + 0.1 * wfloat)).astype(BF16)


def shape(dims, kind):
    return jax.ShapeDtypeStruct(dims, kind)


def call(kernel, outs, *args, far_in=(), far_out=False, scratch=(), aliases=None):
    near, far = pl.BlockSpec(memory_space=pltpu.VMEM), pl.BlockSpec(memory_space=pltpu.HBM)
    return pl.pallas_call(
        kernel,
        out_shape=outs,
        in_specs=[far if i in far_in else near for i in range(len(args))],
        out_specs=[far if far_out else near for _ in outs],
        scratch_shapes=scratch,
        input_output_aliases=aliases or {},
        compiler_params=pltpu.CompilerParams(vmem_limit_bytes=48 * 1024 * 1024),
    )(*args)


def swap(value, axis, k):
    return lax.ppermute(value, axis, [(i, i ^ k) for i in range(lax.axis_size(axis))])


def place():
    rep, shard = lax.axis_index("rep"), lax.axis_index("shard")
    return rep & 1, rep >> 1, shard & 1, shard >> 1


def block(index, size):
    return pl.ds(pl.multiple_of(index * size, size), size)


def contract_kernel(away, acts_ref, cots_ref, out_ref, acts, cots, sems):
    core = place()[0]
    half = 1 - core if away else core
    count = cots.shape[0]
    copies = [pltpu.make_async_copy(acts_ref, acts, sems.at[count])]
    for i in range(count):
        source = cots_ref.at[:, block(half * count + i, CHUNK)]
        copies.append(pltpu.make_async_copy(source, cots.at[i], sems.at[i]))
    for copy in copies:
        copy.start()
    copies[0].wait()
    turned = acts[...].T
    for i in range(count):
        copies[i + 1].wait()
        term = jnp.dot(turned, cots[i], preferred_element_type=F32)
        out_ref[:, i * CHUNK:(i + 1) * CHUNK] = term.astype(out_ref.dtype)


def contract(away, acts, cots, kind):
    tokens, rows = acts.shape
    half = cots.shape[1] // 2
    count = half // CHUNK
    return call(
        functools.partial(contract_kernel, away),
        [shape((rows, half), kind)], acts, cots, far_in=(0, 1),
        scratch=[
            pltpu.VMEM((tokens, rows), BF16),
            pltpu.VMEM((count, tokens, CHUNK), BF16),
            pltpu.SemaphoreType.DMA((count + 1,)),
        ],
    )[0]


def first_kernel(rows, kept, came, a_keep, a_send, b_keep, b_send):
    _, x, y, _ = place()
    quarter = a_keep.shape[1]
    for out, side in ((a_keep, x), (a_send, 1 - x)):
        at = block(side, quarter)
        out[...] = (kept[:, at] + came[:, at].astype(F32)).astype(out.dtype)
    for out, side in ((b_keep, y), (b_send, 1 - y)):
        for z in range(out.shape[0] // rows):
            at = block(2 * z + side, rows)
            total = kept[at, 2 * quarter:] + came[at, 2 * quarter:].astype(F32)
            out[z * rows:(z + 1) * rows, :] = total.astype(out.dtype)


def second_a_kernel(rows, kept, came, keep, send):
    _, _, y, _ = place()
    for out, side in ((keep, y), (send, 1 - y)):
        for z in range(out.shape[0] // rows):
            at = block(2 * z + side, rows)
            out[z * rows:(z + 1) * rows, :] = (kept[at, :] + came[at, :].astype(F32)).astype(out.dtype)


def second_b_kernel(kept, came, keep, send):
    _, x, _, _ = place()
    for out, side in ((keep, x), (send, 1 - x)):
        at = block(side, out.shape[1])
        out[...] = (kept[:, at] + came[:, at].astype(F32)).astype(out.dtype)


def third_kernel(a_kept, a_came, b_kept, b_came, *pieces):
    z = place()[3]
    rows, quarter = pieces[0].shape[0], a_kept.shape[1]
    for k, out in enumerate(pieces):
        at = block(z ^ k, rows)
        out[:, :quarter] = (a_kept[at, :] + a_came[at, :].astype(F32)).astype(out.dtype)
        out[:, quarter:] = (b_kept[at, :] + b_came[at, :].astype(F32)).astype(out.dtype)


def update_kernel(w, m, v, own, *refs):
    pieces, (new_w, grad) = refs[:-2], refs[-2:]
    core, x, _, _ = place()
    total = own[...]
    for ref in pieces:
        total += ref[...].astype(F32)
    grad[...] = total.astype(BF16)
    quarter = total.shape[1] // 2
    for part in range(2):
        mine = slice(part * quarter, (part + 1) * quarter)
        at = block(core * 4 + part * 2 + x, quarter)
        new_m, new_v = adamw_moments(m[:, at], v[:, at], total[:, mine])
        new_w[:, mine] = adamw_weight(w[:, at], new_m, new_v)


def pack_kernel(grad, *refs):
    pieces, (a_out, b_out) = refs[:-2], refs[-2:]
    z = place()[3]
    rows, quarter = grad.shape[0], a_out.shape[1]
    for k, ref in enumerate(pieces):
        at = block(z ^ k, rows)
        a_out[at, :] = ref[:, :quarter]
        b_out[at, :] = ref[:, quarter:]
    tail = a_out.shape[0]
    b_out[tail:tail + rows, :] = grad[:, :quarter]
    b_out[tail + rows:tail + 2 * rows, :] = grad[:, quarter:]


def join_a_kernel(rows, mine, other, out):
    y = place()[2]
    for ref, side in ((mine, y), (other, 1 - y)):
        for z in range(ref.shape[0] // rows):
            out[block(2 * z + side, rows), :] = ref[z * rows:(z + 1) * rows, :]


def join_b_kernel(mine, other, out):
    x = place()[1]
    for ref, side in ((mine, x), (other, 1 - x)):
        out[:, block(side, ref.shape[1])] = ref[:out.shape[0], :]


def half_kernel(rows, a_mine, a_other, b_mine, b_other, g_mine, g_other, out):
    _, x, y, _ = place()
    all_rows, quarter = a_mine.shape
    tail = b_mine.shape[0]
    for ref, grad, side in ((a_mine, g_mine, x), (a_other, g_other, 1 - x)):
        out[:all_rows, block(side, quarter)] = ref[...]
        out[all_rows:, block(side, quarter)] = grad[tail:tail + rows, :]
        out[all_rows:, block(2 + side, quarter)] = grad[tail + rows:, :]
    for ref, side in ((b_mine, y), (b_other, 1 - y)):
        for z in range(tail // rows):
            out[block(2 * z + side, rows), 2 * quarter:] = ref[z * rows:(z + 1) * rows, :]


def write_kernel(away, part, m, v, *refs):
    w_out, m_out, v_out, new_m, new_v, sems = refs[-6:]
    core = place()[0]
    all_rows, half = w_out.shape[0], part.shape[1]
    at = block(1 - core if away else core, half)
    copies = [pltpu.make_async_copy(part.at[pl.ds(0, all_rows), :], w_out.at[:, at], sems.at[0])]
    copies[0].start()
    new_m[...], new_v[...] = adamw_moments(m[:, at], v[:, at], part[all_rows:, :].astype(F32))
    for i, (source, out) in enumerate(((new_m, m_out), (new_v, v_out))):
        copies.append(pltpu.make_async_copy(source, out.at[:, at], sems.at[i + 1]))
        copies[-1].start()
    for copy in copies:
        copy.wait()


def body(hidden_acts, out_cotangent, weight, first_moment, second_moment):
    rows, width = weight.shape
    shard_count = lax.axis_size("shard")
    all_rows = hidden_acts.shape[1]
    some_rows, levels = all_rows // 2, shard_count // 2
    half, quarter = width // 2, width // 8

    came = swap(contract(True, hidden_acts, out_cotangent, BF16), "rep", 1)
    kept = contract(False, hidden_acts, out_cotangent, F32)

    a_keep, a_send, b_keep, b_send = call(
        functools.partial(first_kernel, rows),
        [shape((all_rows, quarter), F32), shape((all_rows, quarter), BF16),
         shape((some_rows, 2 * quarter), F32), shape((some_rows, 2 * quarter), BF16)],
        kept, came,
    )
    a_came, b_came = swap(a_send, "rep", 2), swap(b_send, "shard", 1)
    sizes = [shape((some_rows, quarter), F32), shape((some_rows, quarter), BF16)]
    a_keep, a_send = call(functools.partial(second_a_kernel, rows), sizes, a_keep, a_came)
    b_keep, b_send = call(second_b_kernel, sizes, b_keep, b_came)
    a_came, b_came = swap(a_send, "shard", 1), swap(b_send, "rep", 2)
    own, *pieces = call(
        third_kernel,
        [shape((rows, 2 * quarter), F32)] + [shape((rows, 2 * quarter), BF16)] * (levels - 1),
        a_keep, a_came, b_keep, b_came,
    )
    pieces = [swap(piece, "shard", 2 * (k + 1)) for k, piece in enumerate(pieces)]
    new_w, grad = call(
        update_kernel, [shape((rows, 2 * quarter), BF16)] * 2,
        weight, first_moment, second_moment, own, *pieces,
    )

    pieces = [new_w] + [swap(new_w, "shard", 2 * k) for k in range(1, levels)]
    a_part, b_part = call(
        pack_kernel,
        [shape((some_rows, quarter), BF16), shape((some_rows + 2 * rows, quarter), BF16)],
        grad, *pieces,
    )
    a_other, g_other = swap(a_part, "shard", 1), swap(b_part, "rep", 2)
    a_mine = call(functools.partial(join_a_kernel, rows), [shape((all_rows, quarter), BF16)], a_part, a_other)[0]
    b_mine = call(join_b_kernel, [shape((some_rows, 2 * quarter), BF16)], b_part, g_other)[0]
    a_other, b_other = swap(a_mine, "rep", 2), swap(b_mine, "shard", 1)
    part = call(
        functools.partial(half_kernel, rows), [shape((all_rows + rows, half), BF16)],
        a_mine, a_other, b_mine, b_other, b_part, g_other,
    )[0]
    other = swap(part, "rep", 1)
    results = [shape((all_rows, width), BF16), shape((rows, width), F32), shape((rows, width), F32)]
    scratch = [pltpu.VMEM((rows, half), F32), pltpu.VMEM((rows, half), F32), pltpu.SemaphoreType.DMA((3,))]
    written = call(
        functools.partial(write_kernel, False), results,
        part, first_moment, second_moment, far_out=True, scratch=scratch,
    )
    return tuple(call(
        functools.partial(write_kernel, True), results,
        other, first_moment, second_moment, *written,
        far_in=(3, 4, 5), far_out=True, scratch=scratch, aliases={3: 0, 4: 1, 5: 2},
    ))


def solution(mesh):
    return jax.shard_map(
        body,
        mesh=mesh,
        in_specs=(
            P(("rep", "shard"), None),
            P(("rep", "shard"), None),
            P("shard", None),
            P("shard", None),
            P("shard", None),
        ),
        out_specs=(P(), P("shard", None), P("shard", None)),
        check_vma=False,
    )
```

time: 169 us -> 51.7 us (0.31)
  waiting for transfers between devices: 144 us -> 21.8 us
  starting transfers between devices: 0.12 us -> 20.9 us
  between operations: 13.8 us -> 0.77 us
  Pallas kernels: 0 us -> 7.16 us
  matrix products: 5.14 us -> 0 us
  other arithmetic: 3.48 us -> 0 us
  local copies, waits for them, and re-layouts: 3.15 us -> 0.94 us
    reduce_scatter x1 -> x0, waiting for transfers between devices: 70.6 us -> none  [body(): lax.psum_scatter(contract(hidden_acts, out_cotangent), 'shard', scatter_d...]
    all_gather x1 -> x0, waiting for transfers between devices: 41.2 us -> none  [body(): weights_out = lax.all_gather(new_w, 'shard', axis=0, tiled=True)]
    psum x1 -> x0, waiting for transfers between devices: 31.6 us -> none  [body(): grad = lax.psum(grad.astype(jnp.bfloat16), 'rep').astype(jnp.float32)]
    ppermute x0 -> x16, waiting for transfers between devices: none -> 21.8 us  [swap(): lax.ppermute(value, axis, [(i, i ^ k) for i in range(lax.axis_size(axis))])]
    ppermute x0 -> x16, starting transfers between devices: none -> 20.9 us  [swap(): lax.ppermute(value, axis, [(i, i ^ k) for i in range(lax.axis_size(axis))])]
    pallas_call x0 -> x13, Pallas kernels: none -> 7.16 us  [call(): pl.pallas_call(kernel, out_shape=outs, in_specs=[far if i in far_in else...]
    dot_general x1 -> x0, matrix products: 5.14 us -> none  [contract(): lax.dot_general(acts, cots, (((0,), (0,)), ((), ())), preferred_element_t...]
    convert_element_type x2 -> x0, other arithmetic: 3.48 us -> none  [the longest x1 1.87 us: adamw(): new_weight = (wfloat - 0.05 * (update + 0.1 * wfloat)).astype(jnp.bfloat16)]
  transfers between devices with their start and end apart: 3 -> 16, of which waited for: 3 -> 11; matrix products, arithmetic and copies ran while one was open for 0% -> 0% of each run, Pallas kernels for 0% -> 7%
where the time goes in v2:
time: 51.7 us; the launch traced here: 51.5 us
  waiting for transfers between devices  21.8 us (42%)
  starting transfers between devices  20.9 us (40%)
  Pallas kernels  7.16 us (14%)
  local copies, waits for them, and re-layouts  0.94 us (2%)
  between operations  0.77 us (1%)
    ppermute x16, waiting for transfers between devices, swap(): lax.ppermute(value, axis, [(i, i ^ k) for i in range(lax.axis_size(axis))])  21.8 us
    ppermute x16, starting transfers between devices, swap(): lax.ppermute(value, axis, [(i, i ^ k) for i in range(lax.axis_size(axis))])  20.9 us
    pallas_call x13, Pallas kernels, call(): pl.pallas_call(kernel, out_shape=outs, in_specs=[far if i in far_in else...  7.16 us
  transfers between devices with their start and end apart: 16, of which 11 were waited for; matrix products, arithmetic and copies ran while one was open for 0% of the time, Pallas kernels for 7%

profile of v2, /device:TPU:0, one launch (start us, length us, event | category | flops | bytes accessed | tf_op | source)
XLA Modules:
  0.0 51.5 jit_solution(4725334317803719585)
XLA Ops:
  0.6 0.9 %copy-done.2 = bf16[768,128]{1,0:T(8,128)(2,1)S(1)} copy-done((bf16[768,128]{1,0:T(8,128)(2,1)S(1)}, bf16[768,128]{1,0:T(8,128)(2,1)}, u32[]{:S(2)}) %copy-start.2) | copy-done | bytes 196632
  1.6 2.5 %shard_map.77 = bf16[128,2048]{1,0:T(8,128)(2,1)S(1)} custom-call(bf16[768,128]{1,0:T(8,128)(2,1)S(1)} %copy-done.2, bf16[768,4096]{1,0:T(8,128)(2,1)} %cots_ref.3), custom_call_target="tpu_custom_call" | custom-call | tf_op jit(solution)/shard_map/pallas_call | solution.py:35
  4.6 2.5 %shard_map.76.kept = f32[128,2048]{1,0:T(8,128)S(1)} custom-call(bf16[768,128]{1,0:T(8,128)(2,1)S(1)} %copy-done.2, bf16[768,4096]{1,0:T(8,128)(2,1)} %cots_ref.3), custom_call_target="tpu_custom_call" | custom-call | tf_op jit(solution)/shard_map/pallas_call | solution.py:35
  7.2 2.6 %collective-permute-start.1 = (bf16[128,512]{1,0:T(8,128)(2,1)S(1)}, bf16[128,512]{1,0:T(8,128)(2,1)S(1)}, u32[]{:S(2)}, u32[]{:S(2)}) collective-permute-start(bf16[128,512]{1,0:T(8,128)(2,1)S(1)} %get-tuple-element.23), channel_id=1, source_target_pairs={{0,16},{8,24},{16,0},{24,8},{1,17},{9,25},{17,1},{25,9},{2,18},{10... | collective-permute-start | bytes 393224 | tf_op jit(solution)/shard_map/ppermute | solution.py:47
  9.8 1.5 %collective-permute-start.3 = (bf16[64,1024]{1,0:T(8,128)(2,1)S(1)}, bf16[64,1024]{1,0:T(8,128)(2,1)S(1)}, u32[]{:S(2)}, u32[]{:S(2)}) collective-permute-start(bf16[64,1024]{1,0:T(8,128)(2,1)S(1)} %get-tuple-element.27), channel_id=1, source_target_pairs={{0,1},{1,0},{2,3},{3,2},{4,5},{5,4},{6,7},{7,6},{8,9},{9,8},{10,11... | collective-permute-start | bytes 393224 | tf_op jit(solution)/shard_map/ppermute | solution.py:47
  11.4 2.6 %collective-permute-done.1.came = bf16[128,512]{1,0:T(8,128)(2,1)S(1)} collective-permute-done((bf16[128,512]{1,0:T(8,128)(2,1)S(1)}, bf16[128,512]{1,0:T(8,128)(2,1)S(1)}, u32[]{:S(2)}, u32[]{:S(2)}) %collective-permute-start.1) | collective-permute-done | bytes 131104 | tf_op jit(solution)/shard_map/ppermute | solution.py:47
  14.0 1.8 %collective-permute-start.2 = (bf16[64,512]{1,0:T(8,128)(2,1)S(1)}, bf16[64,512]{1,0:T(8,128)(2,1)S(1)}, u32[]{:S(2)}, u32[]{:S(2)}) collective-permute-start(bf16[64,512]{1,0:T(8,128)(2,1)S(1)} %get-tuple-element.25), channel_id=1, source_target_pairs={{0,1},{1,0},{2,3},{3,2},{4,5},{5,4},{6,7},{7,6},{8,9},{9,8},{10,11... | collective-permute-start | bytes 196616 | tf_op jit(solution)/shard_map/ppermute | solution.py:47
  15.8 1.6 %collective-permute-start.4 = (bf16[64,512]{1,0:T(8,128)(2,1)S(1)}, bf16[64,512]{1,0:T(8,128)(2,1)S(1)}, u32[]{:S(2)}, u32[]{:S(2)}) collective-permute-start(bf16[64,512]{1,0:T(8,128)(2,1)S(1)} %get-tuple-element.29), channel_id=1, source_target_pairs={{0,16},{8,24},{16,0},{24,8},{1,17},{9,25},{17,1},{25,9},{2,18},{10... | collective-permute-start | bytes 196616 | tf_op jit(solution)/shard_map/ppermute | solution.py:47
  17.4 0.9 %collective-permute-done.2.a_came = bf16[64,512]{1,0:T(8,128)(2,1)S(1)} collective-permute-done((bf16[64,512]{1,0:T(8,128)(2,1)S(1)}, bf16[64,512]{1,0:T(8,128)(2,1)S(1)}, u32[]{:S(2)}, u32[]{:S(2)}) %collective-permute-start.2) | collective-permute-done | bytes 65568 | tf_op jit(solution)/shard_map/ppermute | solution.py:47
  18.3 1.9 %collective-permute-done.4.b_came = bf16[64,512]{1,0:T(8,128)(2,1)S(1)} collective-permute-done((bf16[64,512]{1,0:T(8,128)(2,1)S(1)}, bf16[64,512]{1,0:T(8,128)(2,1)S(1)}, u32[]{:S(2)}, u32[]{:S(2)}) %collective-permute-start.4) | collective-permute-done | bytes 65568 | tf_op jit(solution)/shard_map/ppermute | solution.py:47
  20.2 1.6 %collective-permute-start.5 = (bf16[16,1024]{1,0:T(8,128)(2,1)S(1)}, bf16[16,1024]{1,0:T(8,128)(2,1)S(1)}, u32[]{:S(2)}, u32[]{:S(2)}) collective-permute-start(bf16[16,1024]{1,0:T(8,128)(2,1)S(1)} %get-tuple-element.31), channel_id=1, source_target_pairs={{0,2},{1,3},{2,0},{3,1},{4,6},{5,7},{6,4},{7,5},{8,10},{9,11},{10,... | collective-permute-start | bytes 98312 | tf_op jit(solution)/shard_map/ppermute | solution.py:47
  21.8 2.6 %collective-permute-start.6 = (bf16[16,1024]{1,0:T(8,128)(2,1)S(1)}, bf16[16,1024]{1,0:T(8,128)(2,1)S(1)}, u32[]{:S(2)}, u32[]{:S(2)}) collective-permute-start(bf16[16,1024]{1,0:T(8,128)(2,1)S(1)} %get-tuple-element.32), channel_id=1, source_target_pairs={{0,4},{1,5},{2,6},{3,7},{4,0},{5,1},{6,2},{7,3},{8,12},{9,13},{10,... | collective-permute-start | bytes 98312 | tf_op jit(solution)/shard_map/ppermute | solution.py:47
  24.7 2.6 %collective-permute-done.6.refs_1_ = bf16[16,1024]{1,0:T(8,128)(2,1)S(1)} collective-permute-done((bf16[16,1024]{1,0:T(8,128)(2,1)S(1)}, bf16[16,1024]{1,0:T(8,128)(2,1)S(1)}, u32[]{:S(2)}, u32[]{:S(2)}) %collective-permute-start.6) | collective-permute-done | bytes 32800 | tf_op jit(solution)/shard_map/ppermute | solution.py:47
  27.3 2.9 %collective-permute-done.7.refs_2_ = bf16[16,1024]{1,0:T(8,128)(2,1)S(1)} collective-permute-done((bf16[16,1024]{1,0:T(8,128)(2,1)S(1)}, bf16[16,1024]{1,0:T(8,128)(2,1)S(1)}, u32[]{:S(2)}, u32[]{:S(2)}) %collective-permute-start.7) | collective-permute-done | bytes 32800 | tf_op jit(solution)/shard_map/ppermute | solution.py:47
  30.7 4.0 %collective-permute-start.8 = (bf16[16,1024]{1,0:T(8,128)(2,1)S(1)}, bf16[16,1024]{1,0:T(8,128)(2,1)S(1)}, u32[]{:S(2)}, u32[]{:S(2)}) collective-permute-start(bf16[16,1024]{1,0:T(8,128)(2,1)S(1)} %get-tuple-element.35.refs_0_), channel_id=1, source_target_pairs={{0,2},{1,3},{2,0},{3,1},{4,6},{5,7},{6,4},{7,5},{8,10},{9,11},{10,... | collective-permute-start | bytes 98312 | tf_op jit(solution)/shard_map/ppermute | solution.py:47
  34.7 1.3 %collective-permute-done.10.refs_3_ = bf16[16,1024]{1,0:T(8,128)(2,1)S(1)} collective-permute-done((bf16[16,1024]{1,0:T(8,128)(2,1)S(1)}, bf16[16,1024]{1,0:T(8,128)(2,1)S(1)}, u32[]{:S(2)}, u32[]{:S(2)}) %collective-permute-start.10) | collective-permute-done | bytes 32800 | tf_op jit(solution)/shard_map/ppermute | solution.py:47
  36.6 1.6 %collective-permute-start.13 = (bf16[96,512]{1,0:T(8,128)(2,1)S(1)}, bf16[96,512]{1,0:T(8,128)(2,1)S(1)}, u32[]{:S(2)}, u32[]{:S(2)}) collective-permute-start(bf16[96,512]{1,0:T(8,128)(2,1)S(1)} %get-tuple-element.37.mine.g_mine), channel_id=1, source_target_pairs={{0,16},{8,24},{16,0},{24,8},{1,17},{9,25},{17,1},{25,9},{2,18},{10... | collective-permute-start | bytes 294920 | tf_op jit(solution)/shard_map/ppermute | solution.py:47
  38.7 3.8 %collective-permute-done.11.other = bf16[64,512]{1,0:T(8,128)(2,1)S(1)} collective-permute-done((bf16[64,512]{1,0:T(8,128)(2,1)S(1)}, bf16[64,512]{1,0:T(8,128)(2,1)S(1)}, u32[]{:S(2)}, u32[]{:S(2)}) %collective-permute-start.11) | collective-permute-done | bytes 65568 | tf_op jit(solution)/shard_map/ppermute | solution.py:47
  42.5 1.0 %collective-permute-start.12 = (bf16[128,512]{1,0:T(8,128)(2,1)S(1)}, bf16[128,512]{1,0:T(8,128)(2,1)S(1)}, u32[]{:S(2)}, u32[]{:S(2)}) collective-permute-start(bf16[128,512]{1,0:T(8,128)(2,1)S(1)} %shard_map.84.a_mine), channel_id=1, source_target_pairs={{0,16},{8,24},{16,0},{24,8},{1,17},{9,25},{17,1},{25,9},{2,18},{10... | collective-permute-start | bytes 393224 | tf_op jit(solution)/shard_map/ppermute | solution.py:47
  44.3 3.2 %collective-permute-done.12.a_other = bf16[128,512]{1,0:T(8,128)(2,1)S(1)} collective-permute-done((bf16[128,512]{1,0:T(8,128)(2,1)S(1)}, bf16[128,512]{1,0:T(8,128)(2,1)S(1)}, u32[]{:S(2)}, u32[]{:S(2)}) %collective-permute-start.12) | collective-permute-done | bytes 131104 | tf_op jit(solution)/shard_map/ppermute | solution.py:47
  47.5 1.0 %collective-permute-done.14.b_other = bf16[64,1024]{1,0:T(8,128)(2,1)S(1)} collective-permute-done((bf16[64,1024]{1,0:T(8,128)(2,1)S(1)}, bf16[64,1024]{1,0:T(8,128)(2,1)S(1)}, u32[]{:S(2)}, u32[]{:S(2)}) %collective-permute-start.14) | collective-permute-done | bytes 131104 | tf_op jit(solution)/shard_map/ppermute | solution.py:47
  48.6 0.9 %shard_map.87 = (bf16[128,4096]{1,0:T(8,128)(2,1)}, f32[16,4096]{1,0:T(8,128)}, f32[16,4096]{1,0:T(8,128)}) custom-call(bf16[144,2048]{1,0:T(8,128)(2,1)S(1)} %shard_map.86.part, f32[16,4096]{1,0:T(8,128)S(1)} %copy-done, f32[16,4096]{1,0:T(8,128)S(1)} %copy-done.1), custom_call_target="tpu_custom_call" | custom-call | tf_op jit(solution)/shard_map/pallas_call | solution.py:35
  49.5 1.1 %collective-permute-done.15.part = bf16[144,2048]{1,0:T(8,128)(2,1)S(1)} collective-permute-done((bf16[144,2048]{1,0:T(8,128)(2,1)S(1)}, bf16[144,2048]{1,0:T(8,128)(2,1)S(1)}, u32[]{:S(2)}, u32[]{:S(2)}) %collective-permute-start.15) | collective-permute-done | bytes 589856 | tf_op jit(solution)/shard_map/ppermute | solution.py:47
  50.6 0.9 %shard_map.88 = (bf16[128,4096]{1,0:T(8,128)(2,1)}, f32[16,4096]{1,0:T(8,128)}, f32[16,4096]{1,0:T(8,128)}) custom-call(bf16[144,2048]{1,0:T(8,128)(2,1)S(1)} %collective-permute-done.15.part, f32[16,4096]{1,0:T(8,128)S(1)} %copy-done, f32[16,4096]{1,0:T(8,128)S(1)} %copy-done.1, ...), custom_call_target="tpu_custom_call", output_to_operand_aliasing={{0}: (3, {}), {1}: (4, {}), {2}: (5, {})} | custom-call | tf_op jit(solution)/shard_map/pallas_call | solution.py:35
  (29 shorter events, 3.5 us)
Async XLA Ops:
  0.6 0.9 %copy-start.2 = (bf16[768,128]{1,0:T(8,128)(2,1)S(1)}, bf16[768,128]{1,0:T(8,128)(2,1)}, u32[]{:S(2)}) copy-start(bf16[768,128]{1,0:T(8,128)(2,1)} %acts_ref.3) | copy-start | bytes 589828
  4.1 26.1 %copy-start = (f32[16,4096]{1,0:T(8,128)S(1)}, f32[16,4096]{1,0:T(8,128)}, u32[]{:S(2)}) copy-start(f32[16,4096]{1,0:T(8,128)} %m.5) | copy-start | bytes 786436
  4.1 26.1 %copy-start.1 = (f32[16,4096]{1,0:T(8,128)S(1)}, f32[16,4096]{1,0:T(8,128)}, u32[]{:S(2)}) copy-start(f32[16,4096]{1,0:T(8,128)} %v.5) | copy-start | bytes 786436
  4.1 26.1 %copy-start.3 = (bf16[16,4096]{1,0:T(8,128)(2,1)S(1)}, bf16[16,4096]{1,0:T(8,128)(2,1)}, u32[]{:S(2)}) copy-start(bf16[16,4096]{1,0:T(8,128)(2,1)} %w.1) | copy-start | bytes 393220
  4.1 3.0 %collective-permute-start = (bf16[128,2048]{1,0:T(8,128)(2,1)S(1)}, bf16[128,2048]{1,0:T(8,128)(2,1)S(1)}, u32[]{:S(2)}, u32[]{:S(2)}) collective-permute-start(bf16[128,2048]{1,0:T(8,128)(2,1)S(1)} %shard_map.77), channel_id=1, source_target_pairs={{0,8},{8,0},{16,24},{24,16},{1,9},{9,1},{17,25},{25,17},{2,10},{10... | collective-permute-start | bytes 1572872 | tf_op jit(solution)/shard_map/ppermute | solution.py:47
  7.2 6.7 %collective-permute-start.1 = (bf16[128,512]{1,0:T(8,128)(2,1)S(1)}, bf16[128,512]{1,0:T(8,128)(2,1)S(1)}, u32[]{:S(2)}, u32[]{:S(2)}) collective-permute-start(bf16[128,512]{1,0:T(8,128)(2,1)S(1)} %get-tuple-element.23), channel_id=1, source_target_pairs={{0,16},{8,24},{16,0},{24,8},{1,17},{9,25},{17,1},{25,9},{2,18},{10... | collective-permute-start | bytes 393224 | tf_op jit(solution)/shard_map/ppermute | solution.py:47
  9.8 6.0 %collective-permute-start.3 = (bf16[64,1024]{1,0:T(8,128)(2,1)S(1)}, bf16[64,1024]{1,0:T(8,128)(2,1)S(1)}, u32[]{:S(2)}, u32[]{:S(2)}) collective-permute-start(bf16[64,1024]{1,0:T(8,128)(2,1)S(1)} %get-tuple-element.27), channel_id=1, source_target_pairs={{0,1},{1,0},{2,3},{3,2},{4,5},{5,4},{6,7},{7,6},{8,9},{9,8},{10,11... | collective-permute-start | bytes 393224 | tf_op jit(solution)/shard_map/ppermute | solution.py:47
  14.0 4.3 %collective-permute-start.2 = (bf16[64,512]{1,0:T(8,128)(2,1)S(1)}, bf16[64,512]{1,0:T(8,128)(2,1)S(1)}, u32[]{:S(2)}, u32[]{:S(2)}) collective-permute-start(bf16[64,512]{1,0:T(8,128)(2,1)S(1)} %get-tuple-element.25), channel_id=1, source_target_pairs={{0,1},{1,0},{2,3},{3,2},{4,5},{5,4},{6,7},{7,6},{8,9},{9,8},{10,11... | collective-permute-start | bytes 196616 | tf_op jit(solution)/shard_map/ppermute | solution.py:47
  15.8 4.3 %collective-permute-start.4 = (bf16[64,512]{1,0:T(8,128)(2,1)S(1)}, bf16[64,512]{1,0:T(8,128)(2,1)S(1)}, u32[]{:S(2)}, u32[]{:S(2)}) collective-permute-start(bf16[64,512]{1,0:T(8,128)(2,1)S(1)} %get-tuple-element.29), channel_id=1, source_target_pairs={{0,16},{8,24},{16,0},{24,8},{1,17},{9,25},{17,1},{25,9},{2,18},{10... | collective-permute-start | bytes 196616 | tf_op jit(solution)/shard_map/ppermute | solution.py:47
  20.2 4.5 %collective-permute-start.5 = (bf16[16,1024]{1,0:T(8,128)(2,1)S(1)}, bf16[16,1024]{1,0:T(8,128)(2,1)S(1)}, u32[]{:S(2)}, u32[]{:S(2)}) collective-permute-start(bf16[16,1024]{1,0:T(8,128)(2,1)S(1)} %get-tuple-element.31), channel_id=1, source_target_pairs={{0,2},{1,3},{2,0},{3,1},{4,6},{5,7},{6,4},{7,5},{8,10},{9,11},{10,... | collective-permute-start | bytes 98312 | tf_op jit(solution)/shard_map/ppermute | solution.py:47
  21.8 5.4 %collective-permute-start.6 = (bf16[16,1024]{1,0:T(8,128)(2,1)S(1)}, bf16[16,1024]{1,0:T(8,128)(2,1)S(1)}, u32[]{:S(2)}, u32[]{:S(2)}) collective-permute-start(bf16[16,1024]{1,0:T(8,128)(2,1)S(1)} %get-tuple-element.32), channel_id=1, source_target_pairs={{0,4},{1,5},{2,6},{3,7},{4,0},{5,1},{6,2},{7,3},{8,12},{9,13},{10,... | collective-permute-start | bytes 98312 | tf_op jit(solution)/shard_map/ppermute | solution.py:47
  24.4 5.7 %collective-permute-start.7 = (bf16[16,1024]{1,0:T(8,128)(2,1)S(1)}, bf16[16,1024]{1,0:T(8,128)(2,1)S(1)}, u32[]{:S(2)}, u32[]{:S(2)}) collective-permute-start(bf16[16,1024]{1,0:T(8,128)(2,1)S(1)} %get-tuple-element.33), channel_id=1, source_target_pairs={{0,6},{1,7},{2,4},{3,5},{4,2},{5,3},{6,0},{7,1},{8,14},{9,15},{10,... | collective-permute-start | bytes 98312 | tf_op jit(solution)/shard_map/ppermute | solution.py:47
  30.3 5.8 %collective-permute-start.10 = (bf16[16,1024]{1,0:T(8,128)(2,1)S(1)}, bf16[16,1024]{1,0:T(8,128)(2,1)S(1)}, u32[]{:S(2)}, u32[]{:S(2)}) collective-permute-start(bf16[16,1024]{1,0:T(8,128)(2,1)S(1)} %get-tuple-element.35.refs_0_), channel_id=1, source_target_pairs={{0,6},{1,7},{2,4},{3,5},{4,2},{5,3},{6,0},{7,1},{8,14},{9,15},{10,... | collective-permute-start | bytes 98312 | tf_op jit(solution)/shard_map/ppermute | solution.py:47
  30.7 5.3 %collective-permute-start.9 = (bf16[16,1024]{1,0:T(8,128)(2,1)S(1)}, bf16[16,1024]{1,0:T(8,128)(2,1)S(1)}, u32[]{:S(2)}, u32[]{:S(2)}) collective-permute-start(bf16[16,1024]{1,0:T(8,128)(2,1)S(1)} %get-tuple-element.35.refs_0_), channel_id=1, source_target_pairs={{0,4},{1,5},{2,6},{3,7},{4,0},{5,1},{6,2},{7,3},{8,12},{9,13},{10,... | collective-permute-start | bytes 98312 | tf_op jit(solution)/shard_map/ppermute | solution.py:47
  30.7 5.9 %collective-permute-start.8 = (bf16[16,1024]{1,0:T(8,128)(2,1)S(1)}, bf16[16,1024]{1,0:T(8,128)(2,1)S(1)}, u32[]{:S(2)}, u32[]{:S(2)}) collective-permute-start(bf16[16,1024]{1,0:T(8,128)(2,1)S(1)} %get-tuple-element.35.refs_0_), channel_id=1, source_target_pairs={{0,2},{1,3},{2,0},{3,1},{4,6},{5,7},{6,4},{7,5},{8,10},{9,11},{10,... | collective-permute-start | bytes 98312 | tf_op jit(solution)/shard_map/ppermute | solution.py:47
  36.6 6.8 %collective-permute-start.13 = (bf16[96,512]{1,0:T(8,128)(2,1)S(1)}, bf16[96,512]{1,0:T(8,128)(2,1)S(1)}, u32[]{:S(2)}, u32[]{:S(2)}) collective-permute-start(bf16[96,512]{1,0:T(8,128)(2,1)S(1)} %get-tuple-element.37.mine.g_mine), channel_id=1, source_target_pairs={{0,16},{8,24},{16,0},{24,8},{1,17},{9,25},{17,1},{25,9},{2,18},{10... | collective-permute-start | bytes 294920 | tf_op jit(solution)/shard_map/ppermute | solution.py:47
  38.2 4.3 %collective-permute-start.11 = (bf16[64,512]{1,0:T(8,128)(2,1)S(1)}, bf16[64,512]{1,0:T(8,128)(2,1)S(1)}, u32[]{:S(2)}, u32[]{:S(2)}) collective-permute-start(bf16[64,512]{1,0:T(8,128)(2,1)S(1)} %get-tuple-element.36.mine), channel_id=1, source_target_pairs={{0,1},{1,0},{2,3},{3,2},{4,5},{5,4},{6,7},{7,6},{8,9},{9,8},{10,11... | collective-permute-start | bytes 196616 | tf_op jit(solution)/shard_map/ppermute | solution.py:47
  42.5 5.0 %collective-permute-start.12 = (bf16[128,512]{1,0:T(8,128)(2,1)S(1)}, bf16[128,512]{1,0:T(8,128)(2,1)S(1)}, u32[]{:S(2)}, u32[]{:S(2)}) collective-permute-start(bf16[128,512]{1,0:T(8,128)(2,1)S(1)} %shard_map.84.a_mine), channel_id=1, source_target_pairs={{0,16},{8,24},{16,0},{24,8},{1,17},{9,25},{17,1},{25,9},{2,18},{10... | collective-permute-start | bytes 393224 | tf_op jit(solution)/shard_map/ppermute | solution.py:47
  43.5 5.0 %collective-permute-start.14 = (bf16[64,1024]{1,0:T(8,128)(2,1)S(1)}, bf16[64,1024]{1,0:T(8,128)(2,1)S(1)}, u32[]{:S(2)}, u32[]{:S(2)}) collective-permute-start(bf16[64,1024]{1,0:T(8,128)(2,1)S(1)} %shard_map.85.b_mine), channel_id=1, source_target_pairs={{0,1},{1,0},{2,3},{3,2},{4,5},{5,4},{6,7},{7,6},{8,9},{9,8},{10,11... | collective-permute-start | bytes 393224 | tf_op jit(solution)/shard_map/ppermute | solution.py:47
  48.5 2.1 %collective-permute-start.15 = (bf16[144,2048]{1,0:T(8,128)(2,1)S(1)}, bf16[144,2048]{1,0:T(8,128)(2,1)S(1)}, u32[]{:S(2)}, u32[]{:S(2)}) collective-permute-start(bf16[144,2048]{1,0:T(8,128)(2,1)S(1)} %shard_map.86.part), channel_id=1, source_target_pairs={{0,8},{8,0},{16,24},{24,16},{1,9},{9,1},{17,25},{25,17},{2,10},{10... | collective-permute-start | bytes 1769480 | tf_op jit(solution)/shard_map/ppermute | solution.py:47
